TPU v7x, 32 devices: a whole 2x2x4 slice. The times are simulated.
32 devices in a mesh: tx: 16 (over z, y, x), ty: 2 (over core).
Axes of the slice: x: 2, y: 2, z: 4, core: 2. Of those that a mesh axis runs over, the one named last changes fastest.
Arguments:
- forcing: float32 [3, 6, 256, 256], P(None, None, 'tx', 'ty'), may hold values from -6 to 6
- start_state: float32 [3, 6, 256, 256], P(None, None, 'tx', 'ty'), may hold values from -4 to 4
- ice_mask: int32 [256, 256], P('tx', 'ty'), may hold values from 0 to 2
- class_ids: int32 [6, 256, 256], P(None, 'tx', 'ty'), may hold values from 0 to 15
- eta_table: float32 [16], replicated, may hold values from 0.1 to 10
- friction: float32 [256, 256], P('tx', 'ty'), may hold values from 0.3 to 30
Outputs:
- adjoint: float32 [3, 6, 256, 256], P(None, None, 'tx', 'ty')
- residual: float32 [3, 6, 256, 256], P(None, None, 'tx', 'ty')
Inputs may be any that keep to these rules, and one draw needn't show every extreme that they name: `ice_mask`: 0 marks an ocean column, 1 a grounded one, 2 a floating one. `class_ids`: an index into eta_table.
All inputs are finite; a program needn't handle non-finite values.
Results may differ from a plain program's by a relative error of at most 0.00002.
Values sent between devices are 32-bit elements; how exact they have to be, the bound alone decides.
No kernel may reach another device: no remote copies, remote signals or barrier semaphores. Data moves between devices by JAX's collectives and lax.ppermute only.
A program may use at most 64 MiB of HBM per device.

v0:
```python
import jax
import jax.numpy as jnp
from jax import lax
from jax.sharding import PartitionSpec as P

SWEEPS = 2
COARSE_SWEEPS = 4


DAMPING = 0.6
VERTICAL = 2.0
REACTION = 0.05


def extended(block, sides, width):
    for axis, dim in sides:
        count = lax.axis_size(axis)
        forward = [(i, i + 1) for i in range(count - 1)]
        backward = [(target, source) for source, target in forward]
        low = lax.ppermute(
            lax.slice_in_dim(block, block.shape[dim] - width, None, axis=dim), axis, forward
        )
        high = lax.ppermute(lax.slice_in_dim(block, 0, width, axis=dim), axis, backward)
        block = jnp.concatenate([low, block, high], axis=dim)
    return block


def stencil_terms():
    terms = []
    for step_z in (-1, 0, 1):
        for step_x in (-1, 0, 1):
            for step_y in (-1, 0, 1):
                nonzero_axes = abs(step_z) + abs(step_x) + abs(step_y)
                if nonzero_axes > 0:
                    terms.append((step_z, step_x, step_y, nonzero_axes))
    return terms


def apply_operator(padded, coef_pad, spacing, ocean_weight):
    layers = padded.shape[1]
    width_x = padded.shape[2] - 2
    width_y = padded.shape[3] - 2
    viscosity = coef_pad[:layers]
    active = jnp.broadcast_to(coef_pad[layers], viscosity.shape)
    basal = coef_pad[layers + 1]
    visc_z = jnp.pad(viscosity, ((1, 1), (0, 0), (0, 0)))
    active_z = jnp.pad(active, ((1, 1), (0, 0), (0, 0)))
    field_z = jnp.pad(padded, ((0, 0), (1, 1), (0, 0), (0, 0)))
    visc_mid = viscosity[:, 1 : 1 + width_x, 1 : 1 + width_y]
    active_mid = active[:, 1 : 1 + width_x, 1 : 1 + width_y]
    coupled = jnp.zeros((3, layers, width_x, width_y), jnp.float32)
    weight_sum = jnp.zeros((3, layers, width_x, width_y), jnp.float32)
    for step_z, step_x, step_y, nonzero_axes in stencil_terms():
        base_weight = (
            0.25 ** (nonzero_axes - 1)
            * VERTICAL ** abs(step_z)
            * spacing ** (abs(step_x) + abs(step_y))
        )
        factors = (
            jnp.array(
                [1.0 + abs(step_x), 1.0 + abs(step_y), 1.0 + abs(step_z)], jnp.float32
            ).reshape(3, 1, 1, 1)
            * base_weight
        )
        z_range = slice(1 + step_z, 1 + step_z + layers)
        x_range = slice(1 + step_x, 1 + step_x + width_x)
        y_range = slice(1 + step_y, 1 + step_y + width_y)
        pair_mean = (
            0.5
            * (visc_mid + visc_z[z_range, x_range, y_range])
            * active_mid
            * active_z[z_range, x_range, y_range]
        )
        links = factors * pair_mean[None]
        coupled = coupled + links * field_z[:, z_range, x_range, y_range]
        weight_sum = weight_sum + links
    layer_ids = lax.broadcasted_iota(jnp.int32, (3, layers, 1, 1), 1)
    comp_ids = lax.broadcasted_iota(jnp.int32, (3, layers, 1, 1), 0)
    bottom = jnp.where((layer_ids == 0) & (comp_ids < 2), 1.0, 0.0).astype(jnp.float32)
    basal_term = bottom * basal[None, None, 1 : 1 + width_x, 1 : 1 + width_y]
    diagonal = (
        weight_sum
        + (REACTION * visc_mid * active_mid + ocean_weight * (1.0 - active_mid))[None]
        + basal_term
    )
    centre = padded[:, :, 1 : 1 + width_x, 1 : 1 + width_y]
    return (diagonal * centre - coupled, diagonal)


def jacobi_sweep(padded, right_side, coef_pad, spacing, ocean_weight):
    applied, diagonal = apply_operator(padded, coef_pad, spacing, ocean_weight)
    centre = padded[:, :, 1:-1, 1:-1]
    return centre + DAMPING * (right_side - applied) / diagonal


def build_coefficients(class_ids, eta_table, ice_mask, friction):
    levels = lax.broadcasted_iota(jnp.int32, (eta_table.shape[0], 1, 1, 1), 0)
    viscosity = jnp.sum(
        jnp.where(class_ids[None] == levels, eta_table[:, None, None, None], 0.0), axis=0
    )
    active = jnp.where(ice_mask != 0, 1.0, 0.0).astype(jnp.float32)
    basal = jnp.where(ice_mask == 1, friction, 0.0)
    return jnp.concatenate([viscosity, active[None], basal[None]], axis=0)


def coarsen_sum(values):
    leading = values.shape[:-2]
    shaped = values.reshape(leading + (values.shape[-2] // 2, 2, values.shape[-1] // 2, 2))
    return jnp.sum(shaped, axis=(-3, -1))


def coarse_coefficients(coefficients):
    layers = coefficients.shape[0] - 2
    summed = coarsen_sum(coefficients)
    return jnp.concatenate(
        [summed[:layers], 0.25 * summed[layers : layers + 1], summed[layers + 1 :]], axis=0
    )


def refine(values):
    return jnp.repeat(jnp.repeat(values, 2, axis=-2), 2, axis=-1)


def shards(forcing, start_state, ice_mask, class_ids, eta_table, friction):
    coefficients = build_coefficients(class_ids, eta_table, ice_mask, friction)
    coef_pad = extended(coefficients, (("tx", 1), ("ty", 2)), 1)

    def with_rims(iterate):
        return extended(iterate, (("tx", 2), ("ty", 3)), 1)

    def smooth_residual(iterate):
        for sweep_index in range(SWEEPS):
            iterate = jacobi_sweep(with_rims(iterate), forcing, coef_pad, 1.0, 1.0)
        applied, unused_diag = apply_operator(with_rims(iterate), coef_pad, 1.0, 1.0)
        return (iterate, forcing - applied)

    iterate, fine_residual = smooth_residual(start_state)
    coarse_rhs = coarsen_sum(fine_residual)
    coarse_coef = coarse_coefficients(coefficients)
    coarse_pad = extended(coarse_coef, (("tx", 1), ("ty", 2)), 1)
    correction = jnp.zeros_like(coarse_rhs)
    for sweep_index in range(COARSE_SWEEPS):
        correction = jacobi_sweep(
            extended(correction, (("tx", 2), ("ty", 3)), 1), coarse_rhs, coarse_pad, 0.5, 4.0
        )
    iterate = iterate + refine(correction)
    iterate, final_residual = smooth_residual(iterate)
    return (iterate, final_residual)


def solution(mesh):
    return jax.shard_map(
        shards,
        mesh=mesh,
        in_specs=(
            P(None, None, "tx", "ty"),
            P(None, None, "tx", "ty"),
            P("tx", "ty"),
            P(None, "tx", "ty"),
            P(),
            P("tx", "ty"),
        ),
        out_specs=(P(None, None, "tx", "ty"), P(None, None, "tx", "ty")),
        check_vma=False,
    )
```

profile of v0, /device:TPU:9, one launch (start us, length us, event | category | flops | bytes accessed | tf_op | source)
XLA Modules:
  0.0 220.7 jit_solution(17407688019095683954)
XLA Ops:
  0.6 4.0 %collective-permute-start.21 = (f32[3,6,1,64]{3,2,1,0:T(1,128)S(1)}, f32[3,6,1,64]{3,2,1,0:T(1,128)S(1)}, u32[]{:S(2)}, u32[]{:S(2)}) collective-permute-start(f32[3,6,1,64]{3,2,1,0:T(1,128)S(1)} %broadcast.817), channel_id=1, source_target_pairs={{2,0},{4,2},{6,4},{8,6},{10,8},{12,10},{14,12},{16,14},{18,16},{20... | collective-permute-start | bytes 13832 | tf_op jit(solution)/shard_map/ppermute | solution.py:23
  8.1 5.1 %collective-permute-start.5 = (f32[3,6,1,128]{3,2,1,0:T(1,128)}, f32[3,6,1,128]{3,2,1,0:T(1,128)}, u32[]{:S(2)}, u32[]{:S(2)}) collective-permute-start(f32[3,6,1,128]{3,2,1,0:T(1,128)} %get-tuple-element.93), channel_id=1, source_target_pairs={{2,0},{4,2},{6,4},{8,6},{10,8},{12,10},{14,12},{16,14},{18,16},{20... | collective-permute-start | bytes 27656 | tf_op jit(solution)/shard_map/ppermute | solution.py:23
  23.2 3.4 %collective-permute-start.16 = (f32[8,1,64]{2,1,0:T(1,128)S(1)}, f32[8,1,64]{2,1,0:T(1,128)S(1)}, u32[]{:S(2)}, u32[]{:S(2)}) collective-permute-start(f32[8,1,64]{2,1,0:T(1,128)S(1)} %get-tuple-element.168), channel_id=1, source_target_pairs={{0,2},{2,4},{4,6},{6,8},{8,10},{10,12},{12,14},{14,16},{16,18},{18... | collective-permute-start | bytes 6152 | tf_op jit(solution)/shard_map/ppermute | solution.py:20
  26.7 2.7 %collective-permute-done.16 = f32[8,1,64]{2,1,0:T(1,128)S(1)} collective-permute-done((f32[8,1,64]{2,1,0:T(1,128)S(1)}, f32[8,1,64]{2,1,0:T(1,128)S(1)}, u32[]{:S(2)}, u32[]{:S(2)}) %collective-permute-start.16) | collective-permute-done | bytes 2080 | tf_op jit(solution)/shard_map/ppermute | solution.py:20
  29.4 4.6 %collective-permute-start.19 = (f32[8,10,1]{2,0,1:T(8,128)S(1)}, f32[8,10,1]{2,0,1:T(8,128)S(1)}, u32[]{:S(2)}, u32[]{:S(2)}) collective-permute-start(f32[8,10,1]{2,0,1:T(8,128)S(1)} %get-tuple-element.165), channel_id=1, source_target_pairs={{1,0},{3,2},{5,4},{7,6},{9,8},{11,10},{13,12},{15,14},{17,16},{19,... | collective-permute-start | bytes 968 | tf_op jit(solution)/shard_map/ppermute | solution.py:23
  37.3 3.4 %collective-permute-start = (f32[8,1,128]{2,1,0:T(1,128)S(1)}, f32[8,1,128]{2,1,0:T(1,128)S(1)}, u32[]{:S(2)}, u32[]{:S(2)}) collective-permute-start(f32[8,1,128]{2,1,0:T(1,128)S(1)} %get-tuple-element.151), channel_id=1, source_target_pairs={{0,2},{2,4},{4,6},{6,8},{8,10},{10,12},{12,14},{14,16},{16,18},{18... | collective-permute-start | bytes 12296 | tf_op jit(solution)/shard_map/ppermute | solution.py:20
  44.8 2.7 %collective-permute-start.4 = (f32[3,6,1,128]{3,2,1,0:T(1,128)}, f32[3,6,1,128]{3,2,1,0:T(1,128)S(1)}, u32[]{:S(2)}, u32[]{:S(2)}) collective-permute-start(f32[3,6,1,128]{3,2,1,0:T(1,128)} %get-tuple-element.92), channel_id=1, source_target_pairs={{0,2},{2,4},{4,6},{6,8},{8,10},{10,12},{12,14},{14,16},{16,18},{18... | collective-permute-start | bytes 27656 | tf_op jit(solution)/shard_map/ppermute | solution.py:20
  47.6 3.9 %collective-permute-start.3 = (f32[8,18,1]{2,1,0:T(8,128)S(1)}, f32[8,18,1]{2,1,0:T(8,128)S(1)}, u32[]{:S(2)}, u32[]{:S(2)}) collective-permute-start(f32[8,18,1]{2,1,0:T(8,128)S(1)} %get-tuple-element.140), channel_id=1, source_target_pairs={{1,0},{3,2},{5,4},{7,6},{9,8},{11,10},{13,12},{15,14},{17,16},{19,... | collective-permute-start | bytes 1736 | tf_op jit(solution)/shard_map/ppermute | solution.py:23
  66.5 4.3 %collective-permute-start.9 = (f32[3,6,1,128]{3,2,1,0:T(1,128)S(1)}, f32[3,6,1,128]{3,2,1,0:T(1,128)S(1)}, u32[]{:S(2)}, u32[]{:S(2)}) collective-permute-start(f32[3,6,1,128]{3,2,1,0:T(1,128)S(1)} %get-tuple-element.91), channel_id=1, source_target_pairs={{2,0},{4,2},{6,4},{8,6},{10,8},{12,10},{14,12},{16,14},{18,16},{20... | collective-permute-start | bytes 27656 | tf_op jit(solution)/shard_map/ppermute | solution.py:23
  72.9 2.3 %collective-permute-start.23 = (f32[3,6,10,1]{3,1,2,0:T(8,128)S(1)}, f32[3,6,10,1]{3,1,2,0:T(8,128)S(1)}, u32[]{:S(2)}, u32[]{:S(2)}) collective-permute-start(f32[3,6,10,1]{3,1,2,0:T(8,128)S(1)} %get-tuple-element.138), channel_id=1, source_target_pairs={{1,0},{3,2},{5,4},{7,6},{9,8},{11,10},{13,12},{15,14},{17,16},{19,... | collective-permute-start | bytes 2168 | tf_op jit(solution)/shard_map/ppermute | solution.py:23
  77.2 3.5 %collective-permute-start.11 = (f32[3,6,18,1]{3,2,1,0:T(8,128)S(1)}, f32[3,6,18,1]{3,2,1,0:T(8,128)S(1)}, u32[]{:S(2)}, u32[]{:S(2)}) collective-permute-start(f32[3,6,18,1]{3,2,1,0:T(8,128)S(1)} %get-tuple-element.63), channel_id=1, source_target_pairs={{1,0},{3,2},{5,4},{7,6},{9,8},{11,10},{13,12},{15,14},{17,16},{19,... | collective-permute-start | bytes 3896 | tf_op jit(solution)/shard_map/ppermute | solution.py:23
  85.7 4.5 %collective-permute-start.13 = (f32[3,6,1,128]{3,2,1,0:T(1,128)S(1)}, f32[3,6,1,128]{3,2,1,0:T(1,128)S(1)}, u32[]{:S(2)}, u32[]{:S(2)}) collective-permute-start(f32[3,6,1,128]{3,2,1,0:T(1,128)S(1)} %get-tuple-element.89), channel_id=1, source_target_pairs={{2,0},{4,2},{6,4},{8,6},{10,8},{12,10},{14,12},{16,14},{18,16},{20... | collective-permute-start | bytes 27656 | tf_op jit(solution)/shard_map/ppermute | solution.py:23
  93.2 3.2 %collective-permute-done.12 = f32[3,6,1,128]{3,2,1,0:T(1,128)S(1)} collective-permute-done((f32[3,6,1,128]{3,2,1,0:T(1,128)S(1)}, f32[3,6,1,128]{3,2,1,0:T(1,128)S(1)}, u32[]{:S(2)}, u32[]{:S(2)}) %collective-permute-start.12) | collective-permute-done | bytes 9248 | tf_op jit(solution)/shard_map/ppermute | solution.py:20
  96.6 3.5 %collective-permute-start.15 = (f32[3,6,18,1]{3,2,1,0:T(8,128)S(1)}, f32[3,6,18,1]{3,2,1,0:T(8,128)S(1)}, u32[]{:S(2)}, u32[]{:S(2)}) collective-permute-start(f32[3,6,18,1]{3,2,1,0:T(8,128)S(1)} %get-tuple-element.61), channel_id=1, source_target_pairs={{1,0},{3,2},{5,4},{7,6},{9,8},{11,10},{13,12},{15,14},{17,16},{19,... | collective-permute-start | bytes 3896 | tf_op jit(solution)/shard_map/ppermute | solution.py:23
  108.0 3.9 %reduce_sum.28 = f32[3,6,8,64]{1,3,2,0:T(8,128)} reduce(f32[3,6,8,2,64,2]{1,5,4,3,2,0:T(2,128)S(1)} %bitcast.21, f32[]{:T(128)} %constant.22.clone.1), dimensions={3,5}, to_apply=%region_1.2 | reduce | flops 27648 | bytes 184324 | tf_op jit(solution)/shard_map/reduce_sum | solution.py:109
  113.6 3.1 %fusion.313 = f32[3,6,8,64]{3,2,1,0:T(8,128)S(1)} fusion(f32[3,6,8,64]{3,2,1,0:T(8,128)S(1)} %copy.1227, f32[3,6,10,66]{3,2,1,0:T(8,128)} %copy.1220, f32[3,6,8,64]{3,1,2,0:T(8,128)} %get-tuple-element.204, f32[3,6,1,64]{3,2,1,0:T(1,128)} %copy-done.86, f32[3,6,8,64]{3,1,2,0:T(8,128)} %get-tuple-element.131, f32[3,6,8,64]{3,1,2,0:T(8,128)} %get-tuple-element.205, ...), kind=kLoop, calls=%fused_computation.824 | loop fusion | flops 940032 | bytes 685616 | tf_op jit(solution)/shard_map/div | solution.py:93
  118.7 5.2 %collective-permute-start.25 = (f32[3,6,1,64]{3,2,1,0:T(1,128)S(1)}, f32[3,6,1,64]{3,2,1,0:T(1,128)S(1)}, u32[]{:S(2)}, u32[]{:S(2)}) collective-permute-start(f32[3,6,1,64]{3,2,1,0:T(1,128)S(1)} %get-tuple-element.147), channel_id=1, source_target_pairs={{2,0},{4,2},{6,4},{8,6},{10,8},{12,10},{14,12},{16,14},{18,16},{20... | collective-permute-start | bytes 13832 | tf_op jit(solution)/shard_map/ppermute | solution.py:23
  124.7 3.2 %collective-permute-start.27 = (f32[3,6,10,1]{3,1,2,0:T(8,128)S(1)}, f32[3,6,10,1]{3,1,2,0:T(8,128)S(1)}, u32[]{:S(2)}, u32[]{:S(2)}) collective-permute-start(f32[3,6,10,1]{3,1,2,0:T(8,128)S(1)} %get-tuple-element.126), channel_id=1, source_target_pairs={{1,0},{3,2},{5,4},{7,6},{9,8},{11,10},{13,12},{15,14},{17,16},{19,... | collective-permute-start | bytes 2168 | tf_op jit(solution)/shard_map/ppermute | solution.py:23
  134.4 5.7 %collective-permute-start.29 = (f32[3,6,1,64]{3,2,1,0:T(1,128)S(1)}, f32[3,6,1,64]{3,2,1,0:T(1,128)S(1)}, u32[]{:S(2)}, u32[]{:S(2)}) collective-permute-start(f32[3,6,1,64]{3,2,1,0:T(1,128)S(1)} %get-tuple-element.145), channel_id=1, source_target_pairs={{2,0},{4,2},{6,4},{8,6},{10,8},{12,10},{14,12},{16,14},{18,16},{20... | collective-permute-start | bytes 13832 | tf_op jit(solution)/shard_map/ppermute | solution.py:23
  141.0 2.9 %collective-permute-start.31 = (f32[3,6,10,1]{3,1,2,0:T(8,128)S(1)}, f32[3,6,10,1]{3,1,2,0:T(8,128)S(1)}, u32[]{:S(2)}, u32[]{:S(2)}) collective-permute-start(f32[3,6,10,1]{3,1,2,0:T(8,128)S(1)} %get-tuple-element.121), channel_id=1, source_target_pairs={{1,0},{3,2},{5,4},{7,6},{9,8},{11,10},{13,12},{15,14},{17,16},{19,... | collective-permute-start | bytes 2168 | tf_op jit(solution)/shard_map/ppermute | solution.py:23
  148.2 4.0 %collective-permute-start.32 = (f32[3,6,1,64]{3,2,1,0:T(1,128)S(1)}, f32[3,6,1,64]{3,2,1,0:T(1,128)S(1)}, u32[]{:S(2)}, u32[]{:S(2)}) collective-permute-start(f32[3,6,1,64]{3,2,1,0:T(1,128)S(1)} %get-tuple-element.144), channel_id=1, source_target_pairs={{0,2},{2,4},{4,6},{6,8},{8,10},{10,12},{12,14},{14,16},{16,18},{18... | collective-permute-start | bytes 13832 | tf_op jit(solution)/shard_map/ppermute | solution.py:20
  152.2 3.6 %collective-permute-start.33 = (f32[3,6,1,64]{3,2,1,0:T(1,128)S(1)}, f32[3,6,1,64]{3,2,1,0:T(1,128)S(1)}, u32[]{:S(2)}, u32[]{:S(2)}) collective-permute-start(f32[3,6,1,64]{3,2,1,0:T(1,128)S(1)} %get-tuple-element.143), channel_id=1, source_target_pairs={{2,0},{4,2},{6,4},{8,6},{10,8},{12,10},{14,12},{16,14},{18,16},{20... | collective-permute-start | bytes 13832 | tf_op jit(solution)/shard_map/ppermute | solution.py:23
  157.0 3.2 %collective-permute-start.35 = (f32[3,6,10,1]{3,1,2,0:T(8,128)S(1)}, f32[3,6,10,1]{3,1,2,0:T(8,128)S(1)}, u32[]{:S(2)}, u32[]{:S(2)}) collective-permute-start(f32[3,6,10,1]{3,1,2,0:T(8,128)S(1)} %get-tuple-element.116), channel_id=1, source_target_pairs={{1,0},{3,2},{5,4},{7,6},{9,8},{11,10},{13,12},{15,14},{17,16},{19,... | collective-permute-start | bytes 2168 | tf_op jit(solution)/shard_map/ppermute | solution.py:23
  165.8 5.1 %collective-permute-start.37 = (f32[3,6,1,128]{3,2,1,0:T(1,128)S(1)}, f32[3,6,1,128]{3,2,1,0:T(1,128)S(1)}, u32[]{:S(2)}, u32[]{:S(2)}) collective-permute-start(f32[3,6,1,128]{3,2,1,0:T(1,128)S(1)} %get-tuple-element.87), channel_id=1, source_target_pairs={{2,0},{4,2},{6,4},{8,6},{10,8},{12,10},{14,12},{16,14},{18,16},{20... | collective-permute-start | bytes 27656 | tf_op jit(solution)/shard_map/ppermute | solution.py:23
  173.1 4.0 %collective-permute-done.36 = f32[3,6,1,128]{3,2,1,0:T(1,128)S(1)} collective-permute-done((f32[3,6,1,128]{3,2,1,0:T(1,128)S(1)}, f32[3,6,1,128]{3,2,1,0:T(1,128)S(1)}, u32[]{:S(2)}, u32[]{:S(2)}) %collective-permute-start.36) | collective-permute-done | bytes 9248 | tf_op jit(solution)/shard_map/ppermute | solution.py:20
  177.3 3.5 %collective-permute-start.39 = (f32[3,6,18,1]{3,2,1,0:T(8,128)S(1)}, f32[3,6,18,1]{3,2,1,0:T(8,128)S(1)}, u32[]{:S(2)}, u32[]{:S(2)}) collective-permute-start(f32[3,6,18,1]{3,2,1,0:T(8,128)S(1)} %get-tuple-element.59), channel_id=1, source_target_pairs={{1,0},{3,2},{5,4},{7,6},{9,8},{11,10},{13,12},{15,14},{17,16},{19,... | collective-permute-start | bytes 3896 | tf_op jit(solution)/shard_map/ppermute | solution.py:23
  188.9 3.4 %collective-permute-start.40 = (f32[3,6,1,128]{3,2,1,0:T(1,128)S(1)}, f32[3,6,1,128]{3,2,1,0:T(1,128)S(1)}, u32[]{:S(2)}, u32[]{:S(2)}) collective-permute-start(f32[3,6,1,128]{3,2,1,0:T(1,128)S(1)} %get-tuple-element.84), channel_id=1, source_target_pairs={{0,2},{2,4},{4,6},{6,8},{8,10},{10,12},{12,14},{14,16},{16,18},{18... | collective-permute-start | bytes 27656 | tf_op jit(solution)/shard_map/ppermute | solution.py:20
  192.2 2.8 %collective-permute-done.40 = f32[3,6,1,128]{3,2,1,0:T(1,128)S(1)} collective-permute-done((f32[3,6,1,128]{3,2,1,0:T(1,128)S(1)}, f32[3,6,1,128]{3,2,1,0:T(1,128)S(1)}, u32[]{:S(2)}, u32[]{:S(2)}) %collective-permute-start.40) | collective-permute-done | bytes 9248 | tf_op jit(solution)/shard_map/ppermute | solution.py:20
  195.2 3.2 %collective-permute-start.43 = (f32[3,6,18,1]{3,2,1,0:T(8,128)S(1)}, f32[3,6,18,1]{3,2,1,0:T(8,128)S(1)}, u32[]{:S(2)}, u32[]{:S(2)}) collective-permute-start(f32[3,6,18,1]{3,2,1,0:T(8,128)S(1)} %get-tuple-element.57), channel_id=1, source_target_pairs={{1,0},{3,2},{5,4},{7,6},{9,8},{11,10},{13,12},{15,14},{17,16},{19,... | collective-permute-start | bytes 3896 | tf_op jit(solution)/shard_map/ppermute | solution.py:23
  205.5 3.4 %collective-permute-start.44 = (f32[3,6,1,128]{3,2,1,0:T(1,128)S(1)}, f32[3,6,1,128]{3,2,1,0:T(1,128)S(1)}, u32[]{:S(2)}, u32[]{:S(2)}) collective-permute-start(f32[3,6,1,128]{3,2,1,0:T(1,128)S(1)} %get-tuple-element.82), channel_id=1, source_target_pairs={{0,2},{2,4},{4,6},{6,8},{8,10},{10,12},{12,14},{14,16},{16,18},{18... | collective-permute-start | bytes 27656 | tf_op jit(solution)/shard_map/ppermute | solution.py:20
  208.8 2.8 %collective-permute-done.44 = f32[3,6,1,128]{3,2,1,0:T(1,128)S(1)} collective-permute-done((f32[3,6,1,128]{3,2,1,0:T(1,128)S(1)}, f32[3,6,1,128]{3,2,1,0:T(1,128)S(1)}, u32[]{:S(2)}, u32[]{:S(2)}) %collective-permute-start.44) | collective-permute-done | bytes 9248 | tf_op jit(solution)/shard_map/ppermute | solution.py:20
  211.8 3.2 %collective-permute-start.47 = (f32[3,6,18,1]{3,2,1,0:T(8,128)S(1)}, f32[3,6,18,1]{3,2,1,0:T(8,128)S(1)}, u32[]{:S(2)}, u32[]{:S(2)}) collective-permute-start(f32[3,6,18,1]{3,2,1,0:T(8,128)S(1)} %get-tuple-element.55), channel_id=1, source_target_pairs={{1,0},{3,2},{5,4},{7,6},{9,8},{11,10},{13,12},{15,14},{17,16},{19,... | collective-permute-start | bytes 3896 | tf_op jit(solution)/shard_map/ppermute | solution.py:23
  (400 shorter events, 99.9 us)
Async XLA Ops:
  0.6 50.9 %collective-permute-start.21 = (f32[3,6,1,64]{3,2,1,0:T(1,128)S(1)}, f32[3,6,1,64]{3,2,1,0:T(1,128)S(1)}, u32[]{:S(2)}, u32[]{:S(2)}) collective-permute-start(f32[3,6,1,64]{3,2,1,0:T(1,128)S(1)} %broadcast.817), channel_id=1, source_target_pairs={{2,0},{4,2},{6,4},{8,6},{10,8},{12,10},{14,12},{16,14},{18,16},{20... | collective-permute-start | bytes 13832 | tf_op jit(solution)/shard_map/ppermute | solution.py:23
  4.6 48.2 %collective-permute-start.20 = (f32[3,6,1,64]{3,2,1,0:T(1,128)S(1)}, f32[3,6,1,64]{3,2,1,0:T(1,128)S(1)}, u32[]{:S(2)}, u32[]{:S(2)}) collective-permute-start(f32[3,6,1,64]{3,2,1,0:T(1,128)S(1)} %broadcast.817), channel_id=1, source_target_pairs={{0,2},{2,4},{4,6},{6,8},{8,10},{10,12},{12,14},{14,16},{16,18},{18... | collective-permute-start | bytes 13832 | tf_op jit(solution)/shard_map/ppermute | solution.py:20
  8.1 48.2 %collective-permute-start.5 = (f32[3,6,1,128]{3,2,1,0:T(1,128)}, f32[3,6,1,128]{3,2,1,0:T(1,128)}, u32[]{:S(2)}, u32[]{:S(2)}) collective-permute-start(f32[3,6,1,128]{3,2,1,0:T(1,128)} %get-tuple-element.93), channel_id=1, source_target_pairs={{2,0},{4,2},{6,4},{8,6},{10,8},{12,10},{14,12},{16,14},{18,16},{20... | collective-permute-start | bytes 27656 | tf_op jit(solution)/shard_map/ppermute | solution.py:23
  21.3 5.4 %collective-permute-start.17 = (f32[8,1,64]{2,1,0:T(1,128)S(1)}, f32[8,1,64]{2,1,0:T(1,128)S(1)}, u32[]{:S(2)}, u32[]{:S(2)}) collective-permute-start(f32[8,1,64]{2,1,0:T(1,128)S(1)} %get-tuple-element.169), channel_id=1, source_target_pairs={{2,0},{4,2},{6,4},{8,6},{10,8},{12,10},{14,12},{16,14},{18,16},{20... | collective-permute-start | bytes 6152 | tf_op jit(solution)/shard_map/ppermute | solution.py:23
  23.2 6.1 %collective-permute-start.16 = (f32[8,1,64]{2,1,0:T(1,128)S(1)}, f32[8,1,64]{2,1,0:T(1,128)S(1)}, u32[]{:S(2)}, u32[]{:S(2)}) collective-permute-start(f32[8,1,64]{2,1,0:T(1,128)S(1)} %get-tuple-element.168), channel_id=1, source_target_pairs={{0,2},{2,4},{4,6},{6,8},{8,10},{10,12},{12,14},{14,16},{16,18},{18... | collective-permute-start | bytes 6152 | tf_op jit(solution)/shard_map/ppermute | solution.py:20
  29.4 5.9 %collective-permute-start.19 = (f32[8,10,1]{2,0,1:T(8,128)S(1)}, f32[8,10,1]{2,0,1:T(8,128)S(1)}, u32[]{:S(2)}, u32[]{:S(2)}) collective-permute-start(f32[8,10,1]{2,0,1:T(8,128)S(1)} %get-tuple-element.165), channel_id=1, source_target_pairs={{1,0},{3,2},{5,4},{7,6},{9,8},{11,10},{13,12},{15,14},{17,16},{19,... | collective-permute-start | bytes 968 | tf_op jit(solution)/shard_map/ppermute | solution.py:23
  35.3 9.4 %collective-permute-start.1 = (f32[8,1,128]{2,1,0:T(1,128)S(1)}, f32[8,1,128]{2,1,0:T(1,128)S(1)}, u32[]{:S(2)}, u32[]{:S(2)}) collective-permute-start(f32[8,1,128]{2,1,0:T(1,128)S(1)} %get-tuple-element.152), channel_id=1, source_target_pairs={{2,0},{4,2},{6,4},{8,6},{10,8},{12,10},{14,12},{16,14},{18,16},{20... | collective-permute-start | bytes 12296 | tf_op jit(solution)/shard_map/ppermute | solution.py:23
  37.3 10.2 %collective-permute-start = (f32[8,1,128]{2,1,0:T(1,128)S(1)}, f32[8,1,128]{2,1,0:T(1,128)S(1)}, u32[]{:S(2)}, u32[]{:S(2)}) collective-permute-start(f32[8,1,128]{2,1,0:T(1,128)S(1)} %get-tuple-element.151), channel_id=1, source_target_pairs={{0,2},{2,4},{4,6},{6,8},{8,10},{10,12},{12,14},{14,16},{16,18},{18... | collective-permute-start | bytes 12296 | tf_op jit(solution)/shard_map/ppermute | solution.py:20
  44.8 11.5 %collective-permute-start.4 = (f32[3,6,1,128]{3,2,1,0:T(1,128)}, f32[3,6,1,128]{3,2,1,0:T(1,128)S(1)}, u32[]{:S(2)}, u32[]{:S(2)}) collective-permute-start(f32[3,6,1,128]{3,2,1,0:T(1,128)} %get-tuple-element.92), channel_id=1, source_target_pairs={{0,2},{2,4},{4,6},{6,8},{8,10},{10,12},{12,14},{14,16},{16,18},{18... | collective-permute-start | bytes 27656 | tf_op jit(solution)/shard_map/ppermute | solution.py:20
  47.6 5.3 %collective-permute-start.3 = (f32[8,18,1]{2,1,0:T(8,128)S(1)}, f32[8,18,1]{2,1,0:T(8,128)S(1)}, u32[]{:S(2)}, u32[]{:S(2)}) collective-permute-start(f32[8,18,1]{2,1,0:T(8,128)S(1)} %get-tuple-element.140), channel_id=1, source_target_pairs={{1,0},{3,2},{5,4},{7,6},{9,8},{11,10},{13,12},{15,14},{17,16},{19,... | collective-permute-start | bytes 1736 | tf_op jit(solution)/shard_map/ppermute | solution.py:23
  66.5 10.0 %collective-permute-start.9 = (f32[3,6,1,128]{3,2,1,0:T(1,128)S(1)}, f32[3,6,1,128]{3,2,1,0:T(1,128)S(1)}, u32[]{:S(2)}, u32[]{:S(2)}) collective-permute-start(f32[3,6,1,128]{3,2,1,0:T(1,128)S(1)} %get-tuple-element.91), channel_id=1, source_target_pairs={{2,0},{4,2},{6,4},{8,6},{10,8},{12,10},{14,12},{16,14},{18,16},{20... | collective-permute-start | bytes 27656 | tf_op jit(solution)/shard_map/ppermute | solution.py:23
  70.9 6.2 %collective-permute-start.8 = (f32[3,6,1,128]{3,2,1,0:T(1,128)S(1)}, f32[3,6,1,128]{3,2,1,0:T(1,128)S(1)}, u32[]{:S(2)}, u32[]{:S(2)}) collective-permute-start(f32[3,6,1,128]{3,2,1,0:T(1,128)S(1)} %get-tuple-element.90), channel_id=1, source_target_pairs={{0,2},{2,4},{4,6},{6,8},{8,10},{10,12},{12,14},{14,16},{16,18},{18... | collective-permute-start | bytes 27656 | tf_op jit(solution)/shard_map/ppermute | solution.py:20
  72.9 9.1 %collective-permute-start.23 = (f32[3,6,10,1]{3,1,2,0:T(8,128)S(1)}, f32[3,6,10,1]{3,1,2,0:T(8,128)S(1)}, u32[]{:S(2)}, u32[]{:S(2)}) collective-permute-start(f32[3,6,10,1]{3,1,2,0:T(8,128)S(1)} %get-tuple-element.138), channel_id=1, source_target_pairs={{1,0},{3,2},{5,4},{7,6},{9,8},{11,10},{13,12},{15,14},{17,16},{19,... | collective-permute-start | bytes 2168 | tf_op jit(solution)/shard_map/ppermute | solution.py:23
  75.3 6.8 %collective-permute-start.22 = (f32[3,6,10,1]{3,1,2,0:T(8,128)S(1)}, f32[3,6,10,1]{3,1,2,0:T(8,128)S(1)}, u32[]{:S(2)}, u32[]{:S(2)}) collective-permute-start(f32[3,6,10,1]{3,1,2,0:T(8,128)S(1)} %get-tuple-element.137), channel_id=1, source_target_pairs={{0,1},{2,3},{4,5},{6,7},{8,9},{10,11},{12,13},{14,15},{16,17},{18,... | collective-permute-start | bytes 2168 | tf_op jit(solution)/shard_map/ppermute | solution.py:20
  77.2 5.0 %collective-permute-start.11 = (f32[3,6,18,1]{3,2,1,0:T(8,128)S(1)}, f32[3,6,18,1]{3,2,1,0:T(8,128)S(1)}, u32[]{:S(2)}, u32[]{:S(2)}) collective-permute-start(f32[3,6,18,1]{3,2,1,0:T(8,128)S(1)} %get-tuple-element.63), channel_id=1, source_target_pairs={{1,0},{3,2},{5,4},{7,6},{9,8},{11,10},{13,12},{15,14},{17,16},{19,... | collective-permute-start | bytes 3896 | tf_op jit(solution)/shard_map/ppermute | solution.py:23
  85.7 7.5 %collective-permute-start.13 = (f32[3,6,1,128]{3,2,1,0:T(1,128)S(1)}, f32[3,6,1,128]{3,2,1,0:T(1,128)S(1)}, u32[]{:S(2)}, u32[]{:S(2)}) collective-permute-start(f32[3,6,1,128]{3,2,1,0:T(1,128)S(1)} %get-tuple-element.89), channel_id=1, source_target_pairs={{2,0},{4,2},{6,4},{8,6},{10,8},{12,10},{14,12},{16,14},{18,16},{20... | collective-permute-start | bytes 27656 | tf_op jit(solution)/shard_map/ppermute | solution.py:23
  90.2 6.2 %collective-permute-start.12 = (f32[3,6,1,128]{3,2,1,0:T(1,128)S(1)}, f32[3,6,1,128]{3,2,1,0:T(1,128)S(1)}, u32[]{:S(2)}, u32[]{:S(2)}) collective-permute-start(f32[3,6,1,128]{3,2,1,0:T(1,128)S(1)} %get-tuple-element.88), channel_id=1, source_target_pairs={{0,2},{2,4},{4,6},{6,8},{8,10},{10,12},{12,14},{14,16},{16,18},{18... | collective-permute-start | bytes 27656 | tf_op jit(solution)/shard_map/ppermute | solution.py:20
  96.6 5.6 %collective-permute-start.15 = (f32[3,6,18,1]{3,2,1,0:T(8,128)S(1)}, f32[3,6,18,1]{3,2,1,0:T(8,128)S(1)}, u32[]{:S(2)}, u32[]{:S(2)}) collective-permute-start(f32[3,6,18,1]{3,2,1,0:T(8,128)S(1)} %get-tuple-element.61), channel_id=1, source_target_pairs={{1,0},{3,2},{5,4},{7,6},{9,8},{11,10},{13,12},{15,14},{17,16},{19,... | collective-permute-start | bytes 3896 | tf_op jit(solution)/shard_map/ppermute | solution.py:23
  116.8 7.1 %collective-permute-start.24 = (f32[3,6,1,64]{3,2,1,0:T(1,128)S(1)}, f32[3,6,1,64]{3,2,1,0:T(1,128)S(1)}, u32[]{:S(2)}, u32[]{:S(2)}) collective-permute-start(f32[3,6,1,64]{3,2,1,0:T(1,128)S(1)} %get-tuple-element.148), channel_id=1, source_target_pairs={{0,2},{2,4},{4,6},{6,8},{8,10},{10,12},{12,14},{14,16},{16,18},{18... | collective-permute-start | bytes 13832 | tf_op jit(solution)/shard_map/ppermute | solution.py:20
  118.7 5.9 %collective-permute-start.25 = (f32[3,6,1,64]{3,2,1,0:T(1,128)S(1)}, f32[3,6,1,64]{3,2,1,0:T(1,128)S(1)}, u32[]{:S(2)}, u32[]{:S(2)}) collective-permute-start(f32[3,6,1,64]{3,2,1,0:T(1,128)S(1)} %get-tuple-element.147), channel_id=1, source_target_pairs={{2,0},{4,2},{6,4},{8,6},{10,8},{12,10},{14,12},{16,14},{18,16},{20... | collective-permute-start | bytes 13832 | tf_op jit(solution)/shard_map/ppermute | solution.py:23
  132.5 7.7 %collective-permute-start.28 = (f32[3,6,1,64]{3,2,1,0:T(1,128)S(1)}, f32[3,6,1,64]{3,2,1,0:T(1,128)S(1)}, u32[]{:S(2)}, u32[]{:S(2)}) collective-permute-start(f32[3,6,1,64]{3,2,1,0:T(1,128)S(1)} %get-tuple-element.146), channel_id=1, source_target_pairs={{0,2},{2,4},{4,6},{6,8},{8,10},{10,12},{12,14},{14,16},{16,18},{18... | collective-permute-start | bytes 13832 | tf_op jit(solution)/shard_map/ppermute | solution.py:20
  134.4 6.5 %collective-permute-start.29 = (f32[3,6,1,64]{3,2,1,0:T(1,128)S(1)}, f32[3,6,1,64]{3,2,1,0:T(1,128)S(1)}, u32[]{:S(2)}, u32[]{:S(2)}) collective-permute-start(f32[3,6,1,64]{3,2,1,0:T(1,128)S(1)} %get-tuple-element.145), channel_id=1, source_target_pairs={{2,0},{4,2},{6,4},{8,6},{10,8},{12,10},{14,12},{16,14},{18,16},{20... | collective-permute-start | bytes 13832 | tf_op jit(solution)/shard_map/ppermute | solution.py:23
  148.2 7.7 %collective-permute-start.32 = (f32[3,6,1,64]{3,2,1,0:T(1,128)S(1)}, f32[3,6,1,64]{3,2,1,0:T(1,128)S(1)}, u32[]{:S(2)}, u32[]{:S(2)}) collective-permute-start(f32[3,6,1,64]{3,2,1,0:T(1,128)S(1)} %get-tuple-element.144), channel_id=1, source_target_pairs={{0,2},{2,4},{4,6},{6,8},{8,10},{10,12},{12,14},{14,16},{16,18},{18... | collective-permute-start | bytes 13832 | tf_op jit(solution)/shard_map/ppermute | solution.py:20
  152.2 4.7 %collective-permute-start.33 = (f32[3,6,1,64]{3,2,1,0:T(1,128)S(1)}, f32[3,6,1,64]{3,2,1,0:T(1,128)S(1)}, u32[]{:S(2)}, u32[]{:S(2)}) collective-permute-start(f32[3,6,1,64]{3,2,1,0:T(1,128)S(1)} %get-tuple-element.143), channel_id=1, source_target_pairs={{2,0},{4,2},{6,4},{8,6},{10,8},{12,10},{14,12},{16,14},{18,16},{20... | collective-permute-start | bytes 13832 | tf_op jit(solution)/shard_map/ppermute | solution.py:23
  157.0 4.5 %collective-permute-start.35 = (f32[3,6,10,1]{3,1,2,0:T(8,128)S(1)}, f32[3,6,10,1]{3,1,2,0:T(8,128)S(1)}, u32[]{:S(2)}, u32[]{:S(2)}) collective-permute-start(f32[3,6,10,1]{3,1,2,0:T(8,128)S(1)} %get-tuple-element.116), channel_id=1, source_target_pairs={{1,0},{3,2},{5,4},{7,6},{9,8},{11,10},{13,12},{15,14},{17,16},{19,... | collective-permute-start | bytes 2168 | tf_op jit(solution)/shard_map/ppermute | solution.py:23
  165.8 7.3 %collective-permute-start.37 = (f32[3,6,1,128]{3,2,1,0:T(1,128)S(1)}, f32[3,6,1,128]{3,2,1,0:T(1,128)S(1)}, u32[]{:S(2)}, u32[]{:S(2)}) collective-permute-start(f32[3,6,1,128]{3,2,1,0:T(1,128)S(1)} %get-tuple-element.87), channel_id=1, source_target_pairs={{2,0},{4,2},{6,4},{8,6},{10,8},{12,10},{14,12},{16,14},{18,16},{20... | collective-permute-start | bytes 27656 | tf_op jit(solution)/shard_map/ppermute | solution.py:23
  170.9 6.2 %collective-permute-start.36 = (f32[3,6,1,128]{3,2,1,0:T(1,128)S(1)}, f32[3,6,1,128]{3,2,1,0:T(1,128)S(1)}, u32[]{:S(2)}, u32[]{:S(2)}) collective-permute-start(f32[3,6,1,128]{3,2,1,0:T(1,128)S(1)} %get-tuple-element.86), channel_id=1, source_target_pairs={{0,2},{2,4},{4,6},{6,8},{8,10},{10,12},{12,14},{14,16},{16,18},{18... | collective-permute-start | bytes 27656 | tf_op jit(solution)/shard_map/ppermute | solution.py:20
  177.3 4.8 %collective-permute-start.39 = (f32[3,6,18,1]{3,2,1,0:T(8,128)S(1)}, f32[3,6,18,1]{3,2,1,0:T(8,128)S(1)}, u32[]{:S(2)}, u32[]{:S(2)}) collective-permute-start(f32[3,6,18,1]{3,2,1,0:T(8,128)S(1)} %get-tuple-element.59), channel_id=1, source_target_pairs={{1,0},{3,2},{5,4},{7,6},{9,8},{11,10},{13,12},{15,14},{17,16},{19,... | collective-permute-start | bytes 3896 | tf_op jit(solution)/shard_map/ppermute | solution.py:23
  186.9 5.3 %collective-permute-start.41 = (f32[3,6,1,128]{3,2,1,0:T(1,128)S(1)}, f32[3,6,1,128]{3,2,1,0:T(1,128)S(1)}, u32[]{:S(2)}, u32[]{:S(2)}) collective-permute-start(f32[3,6,1,128]{3,2,1,0:T(1,128)S(1)} %get-tuple-element.85), channel_id=1, source_target_pairs={{2,0},{4,2},{6,4},{8,6},{10,8},{12,10},{14,12},{16,14},{18,16},{20... | collective-permute-start | bytes 27656 | tf_op jit(solution)/shard_map/ppermute | solution.py:23
  188.9 6.2 %collective-permute-start.40 = (f32[3,6,1,128]{3,2,1,0:T(1,128)S(1)}, f32[3,6,1,128]{3,2,1,0:T(1,128)S(1)}, u32[]{:S(2)}, u32[]{:S(2)}) collective-permute-start(f32[3,6,1,128]{3,2,1,0:T(1,128)S(1)} %get-tuple-element.84), channel_id=1, source_target_pairs={{0,2},{2,4},{4,6},{6,8},{8,10},{10,12},{12,14},{14,16},{16,18},{18... | collective-permute-start | bytes 27656 | tf_op jit(solution)/shard_map/ppermute | solution.py:20
  203.5 5.3 %collective-permute-start.45 = (f32[3,6,1,128]{3,2,1,0:T(1,128)S(1)}, f32[3,6,1,128]{3,2,1,0:T(1,128)S(1)}, u32[]{:S(2)}, u32[]{:S(2)}) collective-permute-start(f32[3,6,1,128]{3,2,1,0:T(1,128)S(1)} %get-tuple-element.83), channel_id=1, source_target_pairs={{2,0},{4,2},{6,4},{8,6},{10,8},{12,10},{14,12},{16,14},{18,16},{20... | collective-permute-start | bytes 27656 | tf_op jit(solution)/shard_map/ppermute | solution.py:23
  205.5 6.2 %collective-permute-start.44 = (f32[3,6,1,128]{3,2,1,0:T(1,128)S(1)}, f32[3,6,1,128]{3,2,1,0:T(1,128)S(1)}, u32[]{:S(2)}, u32[]{:S(2)}) collective-permute-start(f32[3,6,1,128]{3,2,1,0:T(1,128)S(1)} %get-tuple-element.82), channel_id=1, source_target_pairs={{0,2},{2,4},{4,6},{6,8},{8,10},{10,12},{12,14},{14,16},{16,18},{18... | collective-permute-start | bytes 27656 | tf_op jit(solution)/shard_map/ppermute | solution.py:20
  (119 other events, 2690.9 us)
where the time goes:
time: 222 us; the launch traced here: 221 us
  starting transfers between devices  132 us (59%)
  waiting for transfers between devices  37.4 us (17%)
  other arithmetic  33.5 us (15%)
  local copies, waits for them, and re-layouts  14.3 us (6%)
  between operations  3.52 us (2%)
    ppermute x24, starting transfers between devices, extended(): lax.ppermute(lax.slice_in_dim(block, 0, width, axis=dim), axis, backward)  84.4 us
    ppermute x24, starting transfers between devices, extended(): lax.ppermute(lax.slice_in_dim(block, block.shape[dim] - width, None, axis...  47.6 us
    ppermute x24, waiting for transfers between devices, extended(): lax.ppermute(lax.slice_in_dim(block, block.shape[dim] - width, None, axis...  34.8 us
    concatenate x32, other arithmetic, extended(): block = jnp.concatenate([low, block, high], axis=dim)  7.84 us
    add x7, other arithmetic, jacobi_sweep(): return centre + DAMPING * (right_side - applied) / diagonal  7.04 us
    reduce_sum x2, other arithmetic, coarsen_sum(): return jnp.sum(shaped, axis=(-3, -1))  6.13 us
  transfers between devices with their start and end apart: 48, of which 19 were waited for; matrix products, arithmetic and copies ran while one was open for 8% of the time, Pallas kernels for 0%

commit v1 on v0

v1 whole, which is shorter than its diff:
```python
import functools

import jax
import jax.numpy as jnp
from jax import lax
from jax.experimental import pallas as pl
from jax.experimental.pallas import tpu as pltpu
from jax.sharding import PartitionSpec as P

DAMPING = 0.6
REACTION = 0.05
F32 = jnp.float32
VMEM = pl.BlockSpec(memory_space=pltpu.VMEM)
SMEM = pl.BlockSpec(memory_space=pltpu.SMEM)
PARAMS = pltpu.CompilerParams(vmem_limit_bytes=16 * 2**20)

REACH, REACH_RHS, REACH_CRHS, REACH_CCOEF = 3, 2, 5, 6


def along_x(block_a, block_b, sizes):
    count, width = sizes
    pairs = []
    for core in range(width):
        step = [(i * width + core, (i + 1) * width + core) for i in range(count - 1)]
        pairs += step if core % 2 == 0 else [(b, a) for a, b in step]
    if width % 2 == 0:
        for core in range(0, width, 2):
            last = (count - 1) * width
            pairs += [(last + core, last + core + 1), (core + 1, core)]
    back = [(b, a) for a, b in pairs]
    return (
        lax.ppermute(block_a, ("tx", "ty"), pairs),
        lax.ppermute(block_b, ("tx", "ty"), back),
    )


def along_y(block, sizes):
    width = sizes[1]
    if width == 1:
        return jnp.zeros_like(block)
    if width == 2:
        return lax.ppermute(block, "ty", [(0, 1), (1, 0)])
    following = lax.ppermute(block, "ty", [(j + 1, j) for j in range(width - 1)])
    previous = lax.ppermute(block, "ty", [(j, j + 1) for j in range(width - 1)])
    lane = lax.broadcasted_iota(jnp.int32, block.shape, block.ndim - 1)
    return jnp.where(lane < block.shape[-1] // 2, following, previous)


def filter_x(value, weight):
    rows = value.shape[0]
    return value + weight * (pltpu.roll(value, 1, 0) + pltpu.roll(value, rows - 1, 0))


def filter_y(pair, weight, step):
    own, halo = pair
    lanes = own.shape[1]
    lane = lax.broadcasted_iota(jnp.int32, own.shape, 1)
    low = lane < step
    high = lane >= lanes - step
    own_low, halo_low = pltpu.roll(own, step, 1), pltpu.roll(halo, step, 1)
    own_high, halo_high = pltpu.roll(own, lanes - step, 1), pltpu.roll(halo, lanes - step, 1)
    new_own = jnp.where(low, halo_low, own_low) + jnp.where(high, halo_high, own_high)
    new_halo = jnp.where(low, own_low, halo_low) + jnp.where(high, own_high, halo_high)
    return own + weight * new_own, halo + weight * new_halo


def filter_z(values, z, weight):
    total = None
    for other in (z - 1, z + 1):
        if 0 <= other < len(values):
            total = values[other] if total is None else total + values[other]
    return values[z] + weight * total


def coupling(c, u, v, va, a, spacing, step):
    layers = len(u)
    wx, wy, wz = (
        jnp.where(c == axis, 2.0, 1.0).astype(F32) * base
        for axis, base in ((0, 0.25 * spacing), (1, 0.25 * spacing), (2, 0.5))
    )
    q = [[va[z][t] * u[z][t] for t in (0, 1)] for z in range(layers)]
    result = []
    for z in range(layers):
        sp, sq = [], []
        for t in (0, 1):
            sp.append(filter_x(a[t] * filter_z([w[t] for w in u], z, wz), wx))
            sq.append(filter_x(filter_z([w[t] for w in q], z, wz), wx))
        sp, sq = filter_y(sp, wy, step), filter_y(sq, wy, step)
        result.append([v[z][t] * sp[t] + sq[t] - 2.0 * q[z][t] for t in (0, 1)])
    return result


def layers_of(ref, c, layers):
    return [[ref[t, c, z] for t in (0, 1)] for z in range(layers)]


def fields_of(ref, layers):
    return [[ref[t, z] for t in (0, 1)] for z in range(layers)]


def build_diagonal(v, va, a, basal, spacing, step, ocean, write):
    layers = len(v)
    ones = [[jnp.ones_like(a[t]) for t in (0, 1)] for _ in range(layers)]

    def component(c, carry):
        terms = coupling(c, ones, v, va, a, spacing, step)
        grounded = jnp.where(c < 2, 1.0, 0.0).astype(F32)
        for z in range(layers):
            for t in (0, 1):
                diagonal = 2.0 * a[t] * terms[z][t] + REACTION * va[z][t] + ocean * (1.0 - a[t])
                if z == 0:
                    diagonal = diagonal + grounded * basal[t]
                write(t, c, z, diagonal)
        return carry

    lax.fori_loop(0, 3, component, 0)


def sweep(source, target, gain, rhs, v_ref, va_ref, a_ref, layers, spacing, step):
    def component(c, carry):
        a = [a_ref[t] for t in (0, 1)]
        u = layers_of(source, c, layers)
        terms = coupling(c, u, fields_of(v_ref, layers), fields_of(va_ref, layers), a, spacing, step)
        for z in range(layers):
            for t in (0, 1):
                applied = rhs[t, c, z] + 2.0 * a[t] * terms[z][t]
                target[t, c, z] = (1.0 - DAMPING) * u[z][t] + gain[t, c, z] * applied
        return carry

    lax.fori_loop(0, 3, component, 0)


def residual(source, rhs, diag, v_ref, va_ref, a_ref, layers, rows, tiles, write):
    def component(c, carry):
        a = [a_ref[t] for t in (0, 1)]
        u = layers_of(source, c, layers)
        terms = coupling(c, u, fields_of(v_ref, layers), fields_of(va_ref, layers), a, 1.0, 1)
        for z in range(layers):
            for t in range(tiles):
                applied = rhs[t, c, z] + 2.0 * a[t] * terms[z][t]
                write(t, c, z, applied[:rows] - diag[t, c, z, :rows] * u[z][t][:rows])
        return carry

    lax.fori_loop(0, 3, component, 0)


def inside(rows, own_rows, lanes, sizes):
    i, j = lax.axis_index("tx"), lax.axis_index("ty")
    below = jnp.where(i < sizes[0] - 1, 1.0, 0.0).astype(F32)
    above = jnp.where(i > 0, 1.0, 0.0).astype(F32)
    after = jnp.where(j < sizes[1] - 1, 1.0, 0.0).astype(F32)
    before = jnp.where(j > 0, 1.0, 0.0).astype(F32)
    row = lax.broadcasted_iota(jnp.int32, (rows, lanes), 0)
    lane = lax.broadcasted_iota(jnp.int32, (rows, lanes), 1)
    middle = own_rows + (rows - own_rows) // 2
    by_row = jnp.where(row < own_rows, 1.0, jnp.where(row < middle, below, above))
    by_lane = jnp.where(lane < lanes // 2, after, before)
    return by_row, by_row * by_lane


def sort_sides(blocks, partner_blocks, sides):
    even = lax.axis_index("ty") % 2 == 0
    first, second = blocks[0][...], blocks[1][...]
    sides[0, 0] = jnp.where(even, first, second)
    sides[0, 1] = jnp.where(even, second, first)
    first, second = partner_blocks[0][...], partner_blocks[1][...]
    sides[1, 0] = jnp.where(even, second, first)
    sides[1, 1] = jnp.where(even, first, second)


def write_messages(forward, backward, out_a, out_b):
    even = lax.axis_index("ty") % 2 == 0
    first, second = forward[...], backward[...]
    out_a[...] = jnp.where(even, first, second)
    out_b[...] = jnp.where(even, second, first)


def pack_kernel(start, forcing, mask, classes, eta, friction, out_a, out_b, coef, ends):
    layers, rows = classes.shape[:2]
    fields = 3 * layers
    ids = classes[...]
    viscosity = jnp.zeros(classes.shape, F32)
    for k in range(eta.shape[0]):
        viscosity = jnp.where(ids == k, eta[k], viscosity)
    coef[:layers] = viscosity
    kind = mask[...]
    coef[layers] = jnp.where(kind != 0, 1.0, 0.0).astype(F32)
    coef[layers + 1] = jnp.where(kind == 1, friction[...], 0.0)
    for side in (0, 1):
        def edge(ref, reach, *index):
            first = rows - reach if side == 0 else 0
            return ref[(*index, slice(first, first + reach))]

        place = 0
        for f in range(fields):
            ends[side, place : place + REACH] = edge(start, REACH, f // layers, f % layers)
            place += REACH
        for f in range(fields):
            ends[side, place : place + REACH_RHS] = edge(forcing, REACH_RHS, f // layers, f % layers)
            place += REACH_RHS
        for f in range(layers + 2):
            ends[side, place : place + REACH] = edge(coef, REACH, f)
            place += REACH
    write_messages(ends.at[0], ends.at[1], out_a, out_b)


def presmooth_kernel(
    sizes,
    start, start_n, forcing, forcing_n, coef, coef_n, in_a, in_b, in_an, in_bn,
    pre, crhs, ccoef, rhs, v, va, a, gain, diag, out_a, out_b,
    sides, u0, u1, res, basal, ends,
):
    layers, rows, lanes = start.shape[1:]
    total = rows + 8
    half = rows // 2
    fields = 3 * layers
    sort_sides((in_a, in_b), (in_an, in_bn), sides)

    def fill(target, own, reach, place, *index):
        t = index[0]
        target[(*index, slice(0, rows))] = own
        target[(*index, slice(rows, total))] = jnp.zeros((8, lanes), F32)
        target[(*index, slice(rows, rows + reach))] = sides[t, 1, place : place + reach]
        target[(*index, slice(total - reach, total))] = sides[t, 0, place : place + reach]

    valid = inside(total, rows, lanes, sizes)
    for t in (0, 1):
        s, g, k = ((start, forcing, coef), (start_n, forcing_n, coef_n))[t]
        place = 0
        for f in range(fields):
            c, z = f // layers, f % layers
            fill(u0, s[c, z], REACH, place, t, c, z)
            place += REACH
        for f in range(fields):
            c, z = f // layers, f % layers
            fill(rhs, g[c, z], REACH_RHS, place, t, c, z)
            place += REACH_RHS
        for z in range(layers):
            fill(v, k[z], REACH, place, t, z)
            place += REACH
        fill(a, k[layers], REACH, place, t)
        fill(basal, k[layers + 1], REACH, place + REACH, t)
        a[t] = a[t] * valid[t]
        for z in range(layers):
            va[t, z] = v[t, z] * a[t]

    def keep(t, c, z, diagonal):
        diag[t, c, z] = diagonal
        gain[t, c, z] = DAMPING / diagonal

    pairs_a = [a[t] for t in (0, 1)]
    build_diagonal(
        fields_of(v, layers), fields_of(va, layers), pairs_a,
        [basal[t] for t in (0, 1)], 1.0, 1, 1.0, keep,
    )
    sweep(u0, u1, gain, rhs, v, va, a, layers, 1.0, 1)
    sweep(u1, u0, gain, rhs, v, va, a, layers, 1.0, 1)

    def put(t, c, z, value):
        res[t, c, z] = value

    residual(u0, rhs, diag, v, va, a, layers, rows, 2, put)
    for t in (0, 1):
        for c in range(3):
            for z in range(layers):
                pre[t, c, z] = u0[t, c, z, :rows]

    even = lax.broadcasted_iota(jnp.int32, (half, lanes), 1) % 2 == 0

    def coarsen(ref, *index):
        summed = ref[(*index, pl.ds(0, half, 2))] + ref[(*index, pl.ds(1, half, 2))]
        return summed + jnp.where(even, pltpu.roll(summed, lanes - 1, 1), pltpu.roll(summed, 1, 1))

    for t in (0, 1):
        for c in range(3):
            for z in range(layers):
                crhs[t, c, z] = coarsen(res, t, c, z)
        for z in range(layers):
            ccoef[t, z] = coarsen(v, t, z)
        ccoef[t, layers] = 0.25 * coarsen(a, t)
        ccoef[t, layers + 1] = coarsen(basal, t)

    for side in (0, 1):
        first = rows - REACH if side == 0 else 0
        place = 0
        for f in range(fields):
            ends[side, place : place + REACH] = u0[0, f // layers, f % layers, first : first + REACH]
            place += REACH

        def edge(value, reach):
            return value[half - reach :] if side == 0 else value[:reach]

        for f in range(0, fields, 2):
            one = crhs[0, f // layers, f % layers]
            two = crhs[0, (f + 1) // layers, (f + 1) % layers]
            ends[side, place : place + REACH_CRHS] = edge(jnp.where(even, one, two), REACH_CRHS)
            place += REACH_CRHS
        for f in range(0, layers + 2, 2):
            both = jnp.where(even, ccoef[0, f], ccoef[0, f + 1])
            ends[side, place : place + REACH_CCOEF] = edge(both, REACH_CCOEF)
            place += REACH_CCOEF
    write_messages(ends.at[0], ends.at[1], out_a, out_b)


def coarse_kernel(
    sizes,
    pre, crhs, ccoef, rhs, v, va, a, gain, diag, in_a, in_b, in_an, in_bn,
    adjoint, final,
    sides, u0, u1, cr, cv, cva, ca, cgain, c0, c1, wide,
):
    layers, rows, lanes = pre.shape[2:]
    total = rows + 8
    half = rows // 2
    ctotal = half + 16
    fields = 3 * layers
    sort_sides((in_a, in_b), (in_an, in_bn), sides)
    place_r = REACH * fields
    place_c = place_r + REACH_CRHS * (fields // 2)
    even = lax.broadcasted_iota(jnp.int32, (8, lanes), 1) % 2 == 0

    def unpack(t, side, place, reach):
        both = sides[t, side, place : place + reach]
        first = even[:reach]
        return (
            jnp.where(first, both, pltpu.roll(both, 1, 1)),
            jnp.where(first, pltpu.roll(both, lanes - 1, 1), both),
        )

    def fill(target, own, above, below, *index):
        reach = above.shape[0]
        target[(*index, slice(0, half))] = own
        target[(*index, slice(half, ctotal))] = jnp.zeros((16, lanes), F32)
        target[(*index, slice(half, half + reach))] = below
        target[(*index, slice(ctotal - reach, ctotal))] = above

    valid = inside(ctotal, half, lanes, sizes)
    for t in (0, 1):
        for m in range(fields // 2):
            above = unpack(t, 0, place_r + REACH_CRHS * m, REACH_CRHS)
            below = unpack(t, 1, place_r + REACH_CRHS * m, REACH_CRHS)
            for k in (0, 1):
                c, z = (2 * m + k) // layers, (2 * m + k) % layers
                fill(cr, crhs[t, c, z], above[k], below[k], t, c, z)
        for m in range(layers // 2 + 1):
            above = unpack(t, 0, place_c + REACH_CCOEF * m, REACH_CCOEF)
            below = unpack(t, 1, place_c + REACH_CCOEF * m, REACH_CCOEF)
            for k in (0, 1):
                f = 2 * m + k
                fill(cv, ccoef[t, f], above[k], below[k], t, f)
        ca[t] = cv[t, layers] * valid[t]
        for z in range(layers):
            cva[t, z] = cv[t, z] * ca[t]

    def keep(t, c, z, diagonal):
        value = DAMPING / diagonal
        cgain[t, c, z] = value
        c0[t, c, z] = value * cr[t, c, z]

    build_diagonal(
        fields_of(cv, layers), fields_of(cva, layers), [ca[t] for t in (0, 1)],
        [cv[t, layers + 1] for t in (0, 1)], 0.5, 2, 4.0, keep,
    )
    sweep(c0, c1, cgain, cr, cv, cva, ca, layers, 0.5, 2)
    sweep(c1, c0, cgain, cr, cv, cva, ca, layers, 0.5, 2)
    sweep(c0, c1, cgain, cr, cv, cva, ca, layers, 0.5, 2)

    for t in (0, 1):
        for c in range(3):
            for z in range(layers):
                place = REACH * (c * layers + z)
                u0[t, c, z, :rows] = pre[t, c, z]
                u0[t, c, z, rows:] = jnp.zeros((8, lanes), F32)
                u0[t, c, z, rows : rows + REACH] = sides[t, 1, place : place + REACH]
                u0[t, c, z, total - REACH :] = sides[t, 0, place : place + REACH]
                for phase in (0, 1):
                    wide[pl.ds(phase, half, 2)] = c1[t, c, z, :half]
                    wide[pl.ds(rows + phase, 2, 2)] = c1[t, c, z, half : half + 2]
                    wide[pl.ds(rows + 4 + phase, 2, 2)] = c1[t, c, z, ctotal - 2 :]
                u0[t, c, z] = u0[t, c, z] + wide[...]
    sweep(u0, u1, gain, rhs, v, va, a, layers, 1.0, 1)
    sweep(u1, u0, gain, rhs, v, va, a, layers, 1.0, 1)

    def put(t, c, z, value):
        final[c, z] = value

    residual(u0, rhs, diag, v, va, a, layers, rows, 1, put)
    for c in range(3):
        for z in range(layers):
            adjoint[c, z] = u0[0, c, z, :rows]


def shards(sizes, forcing, start_state, ice_mask, class_ids, eta_table, friction):
    layers, rows, lanes = start_state.shape[1:]
    total, half = rows + 8, rows // 2
    ctotal = half + 16

    def shape(*dims):
        return jax.ShapeDtypeStruct(dims, F32)

    def message(count):
        return shape(-(-count // 8) * 8, lanes)

    def call(body, outs, scratch, *operands):
        specs = [VMEM] * len(operands)
        if body is pack_kernel:
            specs[4] = SMEM
        return pl.pallas_call(
            body,
            out_shape=outs,
            in_specs=specs,
            out_specs=[VMEM] * len(outs),
            scratch_shapes=[pltpu.VMEM(s.shape, F32) for s in scratch],
            compiler_params=PARAMS,
        )(*operands)

    first = message(3 * layers * (REACH + REACH_RHS) + (layers + 2) * REACH)
    second = message(
        3 * layers * REACH + 3 * layers // 2 * REACH_CRHS + (layers + 2) // 2 * REACH_CCOEF
    )

    def both(block):
        return shape(2, *block.shape)

    start_n, forcing_n = along_y(start_state, sizes), along_y(forcing, sizes)
    block_a, block_b, coef = call(
        pack_kernel,
        [first, first, shape(layers + 2, rows, lanes)],
        [both(first)],
        start_state, forcing, ice_mask, class_ids, eta_table, friction,
    )
    in_a, in_b = along_x(block_a, block_b, sizes)
    coef_n = along_y(coef, sizes)
    in_an, in_bn = along_y(in_a, sizes), along_y(in_b, sizes)
    level = shape(2, 3, layers, total, lanes)
    columns = shape(2, layers, total, lanes)
    plane = shape(2, total, lanes)
    *kept, block_a, block_b = call(
        functools.partial(presmooth_kernel, sizes),
        [
            shape(2, 3, layers, rows, lanes),
            shape(2, 3, layers, half, lanes),
            shape(2, layers + 2, half, lanes),
            level, columns, columns, plane, level, level,
            second, second,
        ],
        [both(both(first)), level, level, shape(2, 3, layers, rows, lanes), plane, both(second)],
        start_state, start_n, forcing, forcing_n, coef, coef_n, in_a, in_b, in_an, in_bn,
    )
    in_a, in_b = along_x(block_a, block_b, sizes)
    in_an, in_bn = along_y(in_a, sizes), along_y(in_b, sizes)
    clevel = shape(2, 3, layers, ctotal, lanes)
    own = shape(3, layers, rows, lanes)
    return call(
        functools.partial(coarse_kernel, sizes),
        [own, own],
        [
            both(both(second)), level, level, clevel,
            shape(2, layers + 2, ctotal, lanes), shape(2, layers, ctotal, lanes),
            shape(2, ctotal, lanes), clevel, clevel, clevel, shape(total, lanes),
        ],
        *kept, in_a, in_b, in_an, in_bn,
    )


def solution(mesh):
    sizes = (mesh.shape["tx"], mesh.shape["ty"])

    def block(*operands):
        return tuple(shards(sizes, *operands))

    return jax.shard_map(
        block,
        mesh=mesh,
        in_specs=(
            P(None, None, "tx", "ty"),
            P(None, None, "tx", "ty"),
            P("tx", "ty"),
            P(None, "tx", "ty"),
            P(),
            P("tx", "ty"),
        ),
        out_specs=(P(None, None, "tx", "ty"), P(None, None, "tx", "ty")),
        check_vma=False,
    )
```

time: 222 us -> 33.6 us (0.15)
  starting transfers between devices: 132 us -> 12.3 us
  other arithmetic: 33.5 us -> 0 us
  waiting for transfers between devices: 37.4 us -> 5.82 us
  Pallas kernels: 0 us -> 9.85 us
  local copies, waits for them, and re-layouts: 14.3 us -> 4.66 us
  between operations: 3.52 us -> 0.66 us
    ppermute x48 -> x11, starting transfers between devices: 132 us -> 12.3 us  [the longest x7 7.49 us: along_y(): return lax.ppermute(block, 'ty', [(0, 1), (1, 0)])]
    ppermute x48 -> x11, waiting for transfers between devices: 37.4 us -> 5.82 us  [the longest x7 2.5 us: along_y(): return lax.ppermute(block, 'ty', [(0, 1), (1, 0)])]
    pallas_call x0 -> x3, Pallas kernels: none -> 9.85 us  [call(): pl.pallas_call(body, out_shape=outs, in_specs=specs, out_specs=[VMEM] * l...]
    concatenate x33 -> x0, other arithmetic: 7.85 us -> none  [the longest x32 7.84 us: extended(): block = jnp.concatenate([low, block, high], axis=dim)]
    reduce_sum x3 -> x0, other arithmetic: 7.1 us -> none  [the longest x2 6.13 us: coarsen_sum(): return jnp.sum(shaped, axis=(-3, -1))]
    add x8 -> x0, other arithmetic: 7.07 us -> none  [the longest x7 7.04 us: jacobi_sweep(): return centre + DAMPING * (right_side - applied) / diagonal]
    slice x28 -> x0, local copies, waits for them, and re-layouts: 4.77 us -> none  [the longest x19 2.82 us: extended(): lax.slice_in_dim(block, block.shape[dim] - width, None, axis=dim)]
    mul x13 -> x0, other arithmetic: 3.97 us -> none  [the longest x10 3.81 us: apply_operator(): 0.5 * (visc_mid + visc_z[z_range, x_range, y_range]) * active_mid]
  transfers between devices with their start and end apart: 48 -> 11, of which waited for: 19 -> 6; matrix products, arithmetic and copies ran while one was open for 8% -> 0% of each run, Pallas kernels for 0% -> 2%
where the time goes in v1:
time: 33.6 us; the launch traced here: 33.3 us
  starting transfers between devices  12.3 us (37%)
  Pallas kernels  9.85 us (29%)
  waiting for transfers between devices  5.82 us (17%)
  local copies, waits for them, and re-layouts  4.66 us (14%)
  between operations  0.66 us (2%)
    pallas_call x3, Pallas kernels, call(): pl.pallas_call(body, out_shape=outs, in_specs=specs, out_specs=[VMEM] * l...  9.85 us
    ppermute x7, starting transfers between devices, along_y(): return lax.ppermute(block, 'ty', [(0, 1), (1, 0)])  7.49 us
    ppermute x2, starting transfers between devices, along_x(): lax.ppermute(block_a, ('tx', 'ty'), pairs)  4.78 us
    unnamed x12, local copies, waits for them, and re-layouts  4.66 us
    ppermute x7, waiting for transfers between devices, along_y(): return lax.ppermute(block, 'ty', [(0, 1), (1, 0)])  2.5 us
    ppermute x2, waiting for transfers between devices, along_x(): lax.ppermute(block_b, ('tx', 'ty'), back)  1.99 us
    ppermute x2, waiting for transfers between devices, along_x(): lax.ppermute(block_a, ('tx', 'ty'), pairs)  1.33 us
  transfers between devices with their start and end apart: 11, of which 6 were waited for; matrix products, arithmetic and copies ran while one was open for 0% of the time, Pallas kernels for 2%

profile of v1, /device:TPU:9, one launch (start us, length us, event | category | flops | bytes accessed | tf_op | source)
XLA Modules:
  0.0 33.3 jit_solution(12196544065002889790)
XLA Ops:
  0.6 0.7 %collective-permute-start.1 = (f32[3,6,16,128]{3,2,1,0:T(8,128)}, f32[3,6,16,128]{3,2,1,0:T(8,128)S(1)}, u32[]{:S(2)}, u32[]{:S(2)}) collective-permute-start(f32[3,6,16,128]{3,2,1,0:T(8,128)} %forcing.3), channel_id=1, source_target_pairs={{0,1},{1,0},{2,3},{3,2},{4,5},{5,4},{6,7},{7,6},{8,9},{9,8},{10,11... | collective-permute-start | bytes 442376 | tf_op jit(solution)/shard_map/ppermute | solution.py:42
  1.4 0.1 collective-permute-start
  1.5 0.0 copy-start
  1.5 0.9 %copy-done = f32[3,6,16,128]{3,2,1,0:T(8,128)S(1)} copy-done((f32[3,6,16,128]{3,2,1,0:T(8,128)S(1)}, f32[3,6,16,128]{3,2,1,0:T(8,128)}, u32[]{:S(2)}) %copy-start) | copy-done | bytes 147480
  2.4 0.9 %copy-done.1 = f32[3,6,16,128]{3,2,1,0:T(8,128)S(1)} copy-done((f32[3,6,16,128]{3,2,1,0:T(8,128)S(1)}, f32[3,6,16,128]{3,2,1,0:T(8,128)}, u32[]{:S(2)}) %copy-start.1) | copy-done | bytes 147480
  3.3 0.8 %copy-done.2 = s32[6,16,128]{2,1,0:T(8,128)S(1)} copy-done((s32[6,16,128]{2,1,0:T(8,128)S(1)}, s32[6,16,128]{2,1,0:T(8,128)}, u32[]{:S(2)}) %copy-start.2) | copy-done | bytes 49176
  4.1 0.7 %copy-done.3 = s32[16,128]{1,0:T(8,128)S(1)} copy-done((s32[16,128]{1,0:T(8,128)S(1)}, s32[16,128]{1,0:T(8,128)}, u32[]{:S(2)}) %copy-start.3) | copy-done | bytes 8216
  4.8 0.7 %copy-done.4 = f32[16,128]{1,0:T(8,128)S(1)} copy-done((f32[16,128]{1,0:T(8,128)S(1)}, f32[16,128]{1,0:T(8,128)}, u32[]{:S(2)}) %copy-start.4) | copy-done | bytes 8216
  5.5 0.7 %copy-done.5 = f32[16]{0:T(128)S(1)} copy-done((f32[16]{0:T(128)S(1)}, f32[16]{0:T(128)}, u32[]{:S(2)}) %copy-start.5) | copy-done | bytes 88
  6.1 0.6 %shard_map.77 = (f32[120,128]{1,0:T(8,128)S(1)}, f32[120,128]{1,0:T(8,128)S(1)}, f32[8,16,128]{2,1,0:T(8,128)S(1)}) custom-call(f32[3,6,16,128]{3,2,1,0:T(8,128)S(1)} %copy-done, f32[3,6,16,128]{3,2,1,0:T(8,128)S(1)} %copy-done.1, s32[16,128]{1,0:T(8,128)S(1)} %copy-done.3, s32[6,16,128]{2,1,0:T(8,128)S(1)} %copy-done.2, f32[16]{0:T(128)S(1)} %copy-done.5, ...), custom_call_target="tpu_custom_call" | custom-call | tf_op jit(solution)/shard_map/pallas_call | solution.py:407
  6.8 2.1 %collective-permute-start.3 = (f32[120,128]{1,0:T(8,128)S(1)}, f32[120,128]{1,0:T(8,128)S(1)}, u32[]{:S(2)}, u32[]{:S(2)}) collective-permute-start(f32[120,128]{1,0:T(8,128)S(1)} %get-tuple-element.17), channel_id=1, source_target_pairs={{0,2},{2,4},{4,6},{6,8},{8,10},{10,12},{12,14},{14,16},{16,18},{18... | collective-permute-start | bytes 184328 | tf_op jit(solution)/shard_map/ppermute | solution.py:32
  8.9 0.0 collective-permute-start.4
  8.9 2.2 %collective-permute-start.2 = (f32[8,16,128]{2,1,0:T(8,128)S(1)}, f32[8,16,128]{2,1,0:T(8,128)S(1)}, u32[]{:S(2)}, u32[]{:S(2)}) collective-permute-start(f32[8,16,128]{2,1,0:T(8,128)S(1)} %get-tuple-element.16.coef), channel_id=1, source_target_pairs={{0,1},{1,0},{2,3},{3,2},{4,5},{5,4},{6,7},{7,6},{8,9},{9,8},{10,11... | collective-permute-start | bytes 196616 | tf_op jit(solution)/shard_map/ppermute | solution.py:42
  11.1 0.0 collective-permute-done.3.in_a
  11.1 2.2 %collective-permute-start.5 = (f32[120,128]{1,0:T(8,128)S(1)}, f32[120,128]{1,0:T(8,128)S(1)}, u32[]{:S(2)}, u32[]{:S(2)}) collective-permute-start(f32[120,128]{1,0:T(8,128)S(1)} %collective-permute-done.3.in_a), channel_id=1, source_target_pairs={{0,1},{1,0},{2,3},{3,2},{4,5},{5,4},{6,7},{7,6},{8,9},{9,8},{10,11... | collective-permute-start | bytes 184328 | tf_op jit(solution)/shard_map/ppermute | solution.py:42
  13.3 0.6 %collective-permute-done.4.in_b = f32[120,128]{1,0:T(8,128)S(1)} collective-permute-done((f32[120,128]{1,0:T(8,128)S(1)}, f32[120,128]{1,0:T(8,128)S(1)}, u32[]{:S(2)}, u32[]{:S(2)}) %collective-permute-start.4) | collective-permute-done | bytes 61472 | tf_op jit(solution)/shard_map/ppermute | solution.py:33
  13.8 0.0 collective-permute-start.6
  13.8 0.0 collective-permute-done.2.coef_n
  13.8 0.3 collective-permute-done.5.in_an
  14.2 0.9 %collective-permute-done.6.in_bn = f32[120,128]{1,0:T(8,128)S(1)} collective-permute-done((f32[120,128]{1,0:T(8,128)S(1)}, f32[120,128]{1,0:T(8,128)S(1)}, u32[]{:S(2)}, u32[]{:S(2)}) %collective-permute-start.6) | collective-permute-done | bytes 61472 | tf_op jit(solution)/shard_map/ppermute | solution.py:42
  15.1 0.0 collective-permute-done.1.forcing_n
  15.1 0.0 collective-permute-done.start_n
  15.1 3.1 %shard_map.78 = (f32[2,3,6,16,128]{4,3,2,1,0:T(8,128)S(1)}, f32[2,3,6,8,128]{4,3,2,1,0:T(8,128)S(1)}, f32[2,8,8,128]{3,2,1,0:T(8,128)S(1)}, f32[2,3,6,24,128]{4,...) custom-call(f32[3,6,16,128]{3,2,1,0:T(8,128)S(1)} %copy-done, ...), custom_call_target="tpu_custom_call" | custom-call | tf_op jit(solution)/shard_map/pallas_call | solution.py:407
  18.2 2.7 %collective-permute-start.7 = (f32[128,128]{1,0:T(8,128)S(1)}, f32[128,128]{1,0:T(8,128)S(1)}, u32[]{:S(2)}, u32[]{:S(2)}) collective-permute-start(f32[128,128]{1,0:T(8,128)S(1)} %get-tuple-element.28), channel_id=1, source_target_pairs={{0,2},{2,4},{4,6},{6,8},{8,10},{10,12},{12,14},{14,16},{16,18},{18... | collective-permute-start | bytes 196616 | tf_op jit(solution)/shard_map/ppermute | solution.py:32
  20.9 0.0 collective-permute-start.8
  20.9 1.3 %collective-permute-done.7.in_a = f32[128,128]{1,0:T(8,128)S(1)} collective-permute-done((f32[128,128]{1,0:T(8,128)S(1)}, f32[128,128]{1,0:T(8,128)S(1)}, u32[]{:S(2)}, u32[]{:S(2)}) %collective-permute-start.7) | collective-permute-done | bytes 65568 | tf_op jit(solution)/shard_map/ppermute | solution.py:32
  22.2 2.3 %collective-permute-start.9 = (f32[128,128]{1,0:T(8,128)S(1)}, f32[128,128]{1,0:T(8,128)S(1)}, u32[]{:S(2)}, u32[]{:S(2)}) collective-permute-start(f32[128,128]{1,0:T(8,128)S(1)} %collective-permute-done.7.in_a), channel_id=1, source_target_pairs={{0,1},{1,0},{2,3},{3,2},{4,5},{5,4},{6,7},{7,6},{8,9},{9,8},{10,11... | collective-permute-start | bytes 196616 | tf_op jit(solution)/shard_map/ppermute | solution.py:42
  24.5 1.4 %collective-permute-done.8.in_b = f32[128,128]{1,0:T(8,128)S(1)} collective-permute-done((f32[128,128]{1,0:T(8,128)S(1)}, f32[128,128]{1,0:T(8,128)S(1)}, u32[]{:S(2)}, u32[]{:S(2)}) %collective-permute-start.8) | collective-permute-done | bytes 65568 | tf_op jit(solution)/shard_map/ppermute | solution.py:33
  25.9 0.0 collective-permute-start.10
  25.9 0.0 collective-permute-done.9.in_an
  25.9 1.2 %collective-permute-done.10.in_bn = f32[128,128]{1,0:T(8,128)S(1)} collective-permute-done((f32[128,128]{1,0:T(8,128)S(1)}, f32[128,128]{1,0:T(8,128)S(1)}, u32[]{:S(2)}, u32[]{:S(2)}) %collective-permute-start.10) | collective-permute-done | bytes 65568 | tf_op jit(solution)/shard_map/ppermute | solution.py:42
  27.1 6.1 %shard_map.79 = (f32[3,6,16,128]{3,2,1,0:T(8,128)}, f32[3,6,16,128]{3,2,1,0:T(8,128)}) custom-call(f32[2,3,6,16,128]{4,3,2,1,0:T(8,128)S(1)} %get-tuple-element.19.pre, f32[2,3,6,8,128]{4,3,2,1,0:T(8,128)S(1)} %get-tuple-element.20.crhs, f32[2,8,8,128]{3,2,1,0:T(8,128)S(1)} %get-tuple-element.21.ccoef, f32[2,3,6,24,128]{4,3,2,1,0:T(8,128)S(1)} %get-tuple-element.22.rhs, ...), custom_call_target="tpu_custom_call" | custom-call | tf_op jit(solution)/shard_map/pallas_call | solution.py:407
  (5 shorter events, 0.0 us)
Async XLA Ops:
  0.6 14.5 %collective-permute-start.1 = (f32[3,6,16,128]{3,2,1,0:T(8,128)}, f32[3,6,16,128]{3,2,1,0:T(8,128)S(1)}, u32[]{:S(2)}, u32[]{:S(2)}) collective-permute-start(f32[3,6,16,128]{3,2,1,0:T(8,128)} %forcing.3), channel_id=1, source_target_pairs={{0,1},{1,0},{2,3},{3,2},{4,5},{5,4},{6,7},{7,6},{8,9},{9,8},{10,11... | collective-permute-start | bytes 442376 | tf_op jit(solution)/shard_map/ppermute | solution.py:42
  1.4 13.7 %collective-permute-start = (f32[3,6,16,128]{3,2,1,0:T(8,128)}, f32[3,6,16,128]{3,2,1,0:T(8,128)S(1)}, u32[]{:S(2)}, u32[]{:S(2)}) collective-permute-start(f32[3,6,16,128]{3,2,1,0:T(8,128)} %start.3), channel_id=1, source_target_pairs={{0,1},{1,0},{2,3},{3,2},{4,5},{5,4},{6,7},{7,6},{8,9},{9,8},{10,11... | collective-permute-start | bytes 442376 | tf_op jit(solution)/shard_map/ppermute | solution.py:42
  1.5 0.9 %copy-start = (f32[3,6,16,128]{3,2,1,0:T(8,128)S(1)}, f32[3,6,16,128]{3,2,1,0:T(8,128)}, u32[]{:S(2)}) copy-start(f32[3,6,16,128]{3,2,1,0:T(8,128)} %start.3) | copy-start | bytes 442372
  2.4 0.9 %copy-start.1 = (f32[3,6,16,128]{3,2,1,0:T(8,128)S(1)}, f32[3,6,16,128]{3,2,1,0:T(8,128)}, u32[]{:S(2)}) copy-start(f32[3,6,16,128]{3,2,1,0:T(8,128)} %forcing.3) | copy-start | bytes 442372
  3.3 0.8 %copy-start.2 = (s32[6,16,128]{2,1,0:T(8,128)S(1)}, s32[6,16,128]{2,1,0:T(8,128)}, u32[]{:S(2)}) copy-start(s32[6,16,128]{2,1,0:T(8,128)} %classes.1) | copy-start | bytes 147460
  4.1 0.7 %copy-start.3 = (s32[16,128]{1,0:T(8,128)S(1)}, s32[16,128]{1,0:T(8,128)}, u32[]{:S(2)}) copy-start(s32[16,128]{1,0:T(8,128)} %mask.1) | copy-start | bytes 24580
  4.8 0.7 %copy-start.4 = (f32[16,128]{1,0:T(8,128)S(1)}, f32[16,128]{1,0:T(8,128)}, u32[]{:S(2)}) copy-start(f32[16,128]{1,0:T(8,128)} %friction.1) | copy-start | bytes 24580
  5.5 0.7 %copy-start.5 = (f32[16]{0:T(128)S(1)}, f32[16]{0:T(128)}, u32[]{:S(2)}) copy-start(f32[16]{0:T(128)} %eta.1) | copy-start | bytes 196
  6.8 4.3 %collective-permute-start.3 = (f32[120,128]{1,0:T(8,128)S(1)}, f32[120,128]{1,0:T(8,128)S(1)}, u32[]{:S(2)}, u32[]{:S(2)}) collective-permute-start(f32[120,128]{1,0:T(8,128)S(1)} %get-tuple-element.17), channel_id=1, source_target_pairs={{0,2},{2,4},{4,6},{6,8},{8,10},{10,12},{12,14},{14,16},{16,18},{18... | collective-permute-start | bytes 184328 | tf_op jit(solution)/shard_map/ppermute | solution.py:32
  8.9 5.0 %collective-permute-start.4 = (f32[120,128]{1,0:T(8,128)S(1)}, f32[120,128]{1,0:T(8,128)S(1)}, u32[]{:S(2)}, u32[]{:S(2)}) collective-permute-start(f32[120,128]{1,0:T(8,128)S(1)} %get-tuple-element.18), channel_id=1, source_target_pairs={{2,0},{4,2},{6,4},{8,6},{10,8},{12,10},{14,12},{16,14},{18,16},{20... | collective-permute-start | bytes 184328 | tf_op jit(solution)/shard_map/ppermute | solution.py:33
  8.9 5.0 %collective-permute-start.2 = (f32[8,16,128]{2,1,0:T(8,128)S(1)}, f32[8,16,128]{2,1,0:T(8,128)S(1)}, u32[]{:S(2)}, u32[]{:S(2)}) collective-permute-start(f32[8,16,128]{2,1,0:T(8,128)S(1)} %get-tuple-element.16.coef), channel_id=1, source_target_pairs={{0,1},{1,0},{2,3},{3,2},{4,5},{5,4},{6,7},{7,6},{8,9},{9,8},{10,11... | collective-permute-start | bytes 196616 | tf_op jit(solution)/shard_map/ppermute | solution.py:42
  11.1 3.1 %collective-permute-start.5 = (f32[120,128]{1,0:T(8,128)S(1)}, f32[120,128]{1,0:T(8,128)S(1)}, u32[]{:S(2)}, u32[]{:S(2)}) collective-permute-start(f32[120,128]{1,0:T(8,128)S(1)} %collective-permute-done.3.in_a), channel_id=1, source_target_pairs={{0,1},{1,0},{2,3},{3,2},{4,5},{5,4},{6,7},{7,6},{8,9},{9,8},{10,11... | collective-permute-start | bytes 184328 | tf_op jit(solution)/shard_map/ppermute | solution.py:42
  13.8 1.2 %collective-permute-start.6 = (f32[120,128]{1,0:T(8,128)S(1)}, f32[120,128]{1,0:T(8,128)S(1)}, u32[]{:S(2)}, u32[]{:S(2)}) collective-permute-start(f32[120,128]{1,0:T(8,128)S(1)} %collective-permute-done.4.in_b), channel_id=1, source_target_pairs={{0,1},{1,0},{2,3},{3,2},{4,5},{5,4},{6,7},{7,6},{8,9},{9,8},{10,11... | collective-permute-start | bytes 184328 | tf_op jit(solution)/shard_map/ppermute | solution.py:42
  18.2 4.0 %collective-permute-start.7 = (f32[128,128]{1,0:T(8,128)S(1)}, f32[128,128]{1,0:T(8,128)S(1)}, u32[]{:S(2)}, u32[]{:S(2)}) collective-permute-start(f32[128,128]{1,0:T(8,128)S(1)} %get-tuple-element.28), channel_id=1, source_target_pairs={{0,2},{2,4},{4,6},{6,8},{8,10},{10,12},{12,14},{14,16},{16,18},{18... | collective-permute-start | bytes 196616 | tf_op jit(solution)/shard_map/ppermute | solution.py:32
  20.9 5.0 %collective-permute-start.8 = (f32[128,128]{1,0:T(8,128)S(1)}, f32[128,128]{1,0:T(8,128)S(1)}, u32[]{:S(2)}, u32[]{:S(2)}) collective-permute-start(f32[128,128]{1,0:T(8,128)S(1)} %get-tuple-element.29), channel_id=1, source_target_pairs={{2,0},{4,2},{6,4},{8,6},{10,8},{12,10},{14,12},{16,14},{18,16},{20... | collective-permute-start | bytes 196616 | tf_op jit(solution)/shard_map/ppermute | solution.py:33
  22.2 3.7 %collective-permute-start.9 = (f32[128,128]{1,0:T(8,128)S(1)}, f32[128,128]{1,0:T(8,128)S(1)}, u32[]{:S(2)}, u32[]{:S(2)}) collective-permute-start(f32[128,128]{1,0:T(8,128)S(1)} %collective-permute-done.7.in_a), channel_id=1, source_target_pairs={{0,1},{1,0},{2,3},{3,2},{4,5},{5,4},{6,7},{7,6},{8,9},{9,8},{10,11... | collective-permute-start | bytes 196616 | tf_op jit(solution)/shard_map/ppermute | solution.py:42
  25.9 1.3 %collective-permute-start.10 = (f32[128,128]{1,0:T(8,128)S(1)}, f32[128,128]{1,0:T(8,128)S(1)}, u32[]{:S(2)}, u32[]{:S(2)}) collective-permute-start(f32[128,128]{1,0:T(8,128)S(1)} %collective-permute-done.8.in_b), channel_id=1, source_target_pairs={{0,1},{1,0},{2,3},{3,2},{4,5},{5,4},{6,7},{7,6},{8,9},{9,8},{10,11... | collective-permute-start | bytes 196616 | tf_op jit(solution)/shard_map/ppermute | solution.py:42
